TPU v7x, 32 devices: a whole 2x2x4 slice. The times are simulated.
32 devices in a mesh: sx: 4 (over y, x), sy: 8 (over z, core).
Axes of the slice: x: 2, y: 2, z: 4, core: 2. Of those that a mesh axis runs over, the one named last changes fastest.
Arguments:
- scalar_field: float32 [128, 256, 512], P('sx', 'sy'), may hold values from -4 to 7
- diffusivity: float32 [128, 256, 512], P('sx', 'sy'), may hold values from 0.03 to 0.11
- reaction_rate: float32 [128, 256, 512], P('sx', 'sy'), may hold values from 0.05 to 0.5
- shear_offsets: int32 [4, 256], replicated, may hold values from 0 to 31
- depth_order: int32 [4, 512], replicated, may hold values from 0 to 1
- tf_centres: float32 [8], replicated, may hold values from -2 to 2
- tf_colour: float32 [3, 8], replicated, may hold values from 0.5 to 2
- tf_opacity: float32 [8], replicated, may hold values from 0.001953125 to 0.01953125
Outputs:
- field_out: float32 [128, 256, 512], P('sx', 'sy')
- image: float32 [4, 3, 128, 512], P(None, None, ('sx', 'sy'))
- transmittance: float32 [4, 128, 512], P(None, ('sx', 'sy'))
All inputs are finite; a program needn't handle non-finite values.
Results may differ from a plain program's by a relative error of at most 0.0002.
Values sent between devices are 32-bit elements; how exact they have to be, the bound alone decides.
A program may use at most 128 MiB of HBM per device.

v0:
```python
import functools
import math

import jax
import jax.numpy as jnp
from jax import lax
from jax.experimental import pallas as pl
from jax.experimental.pallas import tpu as pltpu
from jax.sharding import PartitionSpec as P

STEPS = 4
DIFF_GAIN = 0.4
SHARPNESS = 2.0
LOG2E = math.log2(math.e)
SCALE = SHARPNESS * math.sqrt(LOG2E)
MESH = pl.DeviceIdType.MESH
LANES = 128
SUB = 8
UNROLL = 2
WIDE = 2


def conduct(diff, field):
    return diff * (1.0 + DIFF_GAIN * jnp.tanh(field))


def kernel(
    n_x, n_y,
    u_ref, d_ref, r_ref, off_ref, ord_ref, cen_ref, col_ref, opa_ref,
    f_ref, img_ref, tr_ref,
    field, cond, x_lo, x_hi, dx_lo, dx_hi, p_lo, p_hi, y_lo, y_hi,
    dp_lo, dp_hi, dy_lo, dy_hi, del_lo, del_hi, tall, slope,
    part, got, sgn_ref, c2_ref, wop_ref, wcol_ref,
    halo_send, halo_recv, part_send, part_recv, out_sem,
):
    nx, ny, nz = u_ref.shape
    views = ord_ref.shape[0]
    bumps = cen_ref.shape[0]
    ztiles = nz // LANES
    rows = part.shape[4]
    per_group = SUB // rows
    groups = nx // SUB
    ix, iy = lax.axis_index("sx"), lax.axis_index("sy")

    barrier = pltpu.get_barrier_semaphore()
    for hop in range(1, n_y):
        pl.semaphore_signal(
            barrier, inc=1, device_id={"sy": lax.rem(iy + hop, n_y)}, device_id_type=MESH)

    @pl.when(ix > 0)
    def _():
        pl.semaphore_signal(barrier, inc=1, device_id={"sx": ix - 1}, device_id_type=MESH)

    @pl.when(ix < n_x - 1)
    def _():
        pl.semaphore_signal(barrier, inc=1, device_id={"sx": ix + 1}, device_id_type=MESH)

    sides = [
        (ix > 0, {"sx": ix - 1}, 0, 1),
        (ix < n_x - 1, {"sx": ix + 1}, 1, 0),
        (iy > 0, {"sy": iy - 1}, 2, 3),
        (iy < n_y - 1, {"sy": iy + 1}, 3, 2),
    ]
    landings = [x_lo, x_hi, y_lo, y_hi]
    diff_landings = [dx_lo, dx_hi, dy_lo, dy_hi]

    def halo(step, side):
        exists, neighbour, here, there = sides[side]
        if step == STEPS:
            src = [d_ref.at[0], d_ref.at[nx - 1], dp_lo, dp_hi][side]
            dst, own = diff_landings[there], diff_landings[here]
        else:
            now = step % 2
            src = [
                field.at[now, 0, pl.ds(0, ny)], field.at[now, nx - 1, pl.ds(0, ny)],
                p_lo.at[step], p_hi.at[step],
            ][side]
            dst, own = landings[there].at[step], landings[here].at[step]
        go = pltpu.make_async_remote_copy(
            src_ref=src, dst_ref=dst, send_sem=halo_send.at[step, here],
            recv_sem=halo_recv.at[step, there], device_id=neighbour, device_id_type=MESH)
        come = pltpu.make_async_remote_copy(
            src_ref=src, dst_ref=own, send_sem=halo_send.at[step, here],
            recv_sem=halo_recv.at[step, here], device_id=neighbour, device_id_type=MESH)
        return exists, go, come

    def start_halos(step):
        for side in range(4):
            exists, go, _ = halo(step, side)
            pl.when(exists)(go.start)

    def wait_halos(step):
        for side in range(4):
            exists, go, come = halo(step, side)

            @pl.when(exists)
            def _():
                come.wait_recv()
                go.wait_send()

    for side in range(4):
        @pl.when(jnp.logical_not(sides[side][0]))
        def _():
            landings[side][...] = jnp.zeros_like(landings[side])
            diff_landings[side][...] = jnp.zeros_like(diff_landings[side])

    @pl.loop(0, groups)
    def _(block):
        base = pl.multiple_of(block * SUB, SUB)
        for ref, row, out in (
            (u_ref, 0, p_lo.at[0]), (u_ref, ny - 1, p_hi.at[0]),
            (d_ref, 0, dp_lo), (d_ref, ny - 1, dp_hi),
        ):
            out[pl.ds(base, SUB), :] = jnp.concatenate(
                [ref[base + j, row:row + 1, :] for j in range(SUB)], axis=0)

    @pl.loop(0, nx)
    def _(x):
        for t in range(ny // SUB):
            cut = pl.ds(t * SUB, SUB)
            now = u_ref[x, cut, :]
            field[0, x, cut, :] = now
            cond[x, cut, :] = conduct(d_ref[x, cut, :], now)

    arrivals = (n_y - 1) + (ix > 0).astype(jnp.int32) + (ix < n_x - 1).astype(jnp.int32)
    pl.semaphore_wait(barrier, arrivals)
    start_halos(0)
    start_halos(STEPS)

    row_at = lax.broadcasted_iota(jnp.int32, (SUB, nz), 0)
    col_at = lax.broadcasted_iota(jnp.int32, (SUB, nz), 1)

    for step in range(STEPS):
        now, later = step % 2, (step + 1) % 2
        if step:
            @pl.loop(0, nx)
            def _(x):
                for t in range(ny // SUB):
                    cut = pl.ds(t * SUB, SUB)
                    cond[x, cut, :] = conduct(d_ref[x, cut, :], field[now, x, cut, :])

        @pl.loop(0, nx)
        def _(x):
            below, above = jnp.maximum(x - 1, 0), jnp.minimum(x + 1, nx - 1)
            carried = None
            for t in range(ny // SUB):
                cut, shifted = pl.ds(t * SUB, SUB), pl.ds(t * SUB + 1, SUB)
                u, k = field[now, x, cut, :], cond[x, cut, :]
                change = (k + cond[below, cut, :]) * (field[now, below, cut, :] - u)
                change += (k + cond[above, cut, :]) * (field[now, above, cut, :] - u)
                flux = (k + cond[x, shifted, :]) * (field[now, x, shifted, :] - u)
                if t == ny // SUB - 1:
                    flux = jnp.where(row_at == SUB - 1, 0.0, flux)
                turned = pltpu.roll(flux, 1, 0)
                change += flux - jnp.where(row_at == 0, 0.0 if t == 0 else carried, turned)
                carried = turned
                ku = k * u
                right_u, right_k = pltpu.roll(u, nz - 1, 1), pltpu.roll(k, nz - 1, 1)
                flux = jnp.where(col_at == nz - 1, -ku, (k + right_k) * (right_u - u))
                change += flux - jnp.where(col_at == 0, ku, pltpu.roll(flux, 1, 1))
                field[later, x, cut, :] = u + 0.5 * change + r_ref[x, cut, :] * jnp.tanh(u)

        if step == 0:
            wait_halos(STEPS)
        wait_halos(step)
        inner = pl.ds(0, ny)
        for x, land, diff in ((0, x_lo, dx_lo), (nx - 1, x_hi, dx_hi)):
            beside = land[step]
            field[later, x, inner, :] += (
                0.5 * (cond[x, inner, :] + conduct(diff[...], beside))
                * (beside - field[now, x, inner, :]))
        for packed, own, land, diff, out in (
            (p_lo, dp_lo, y_lo, dy_lo, del_lo), (p_hi, dp_hi, y_hi, dy_hi, del_hi),
        ):
            u, beside = packed[step], land[step]
            out[...] = 0.5 * (conduct(own[...], u) + conduct(diff[...], beside)) * (beside - u)

        @pl.loop(0, groups)
        def _(block):
            base = pl.multiple_of(block * SUB, SUB)
            for packed, delta, row in ((p_lo, del_lo, 0), (p_hi, del_hi, ny - 1)):
                extra = delta[pl.ds(base, SUB), :]
                edge = []
                for j in range(SUB):
                    value = field[later, base + j, row:row + 1, :] + extra[j:j + 1, :]
                    field[later, base + j, row:row + 1, :] = value
                    edge.append(value)
                if step < STEPS - 1:
                    packed[step + 1, pl.ds(base, SUB), :] = jnp.concatenate(edge, axis=0)

        if step < STEPS - 1:
            start_halos(step + 1)

    last = STEPS % 2
    out_copy = pltpu.make_async_copy(field.at[last, :, pl.ds(0, ny)], f_ref, out_sem)
    out_copy.start()

    for ref in (tall, slope):
        ref[ztiles] = jnp.zeros_like(ref[ztiles])

    @pl.loop(0, nx)
    def _(x):
        for t in range(ny // SUB):
            value = field[last, x, pl.ds(t * SUB, SUB), :] * SCALE
            rise = jnp.where(col_at == nz - 1, 0.0, pltpu.roll(value, nz - 1, 1)) - value
            for tile in range(ztiles):
                lanes = slice(tile * LANES, (tile + 1) * LANES)
                spot = pl.ds(t * SUB * nx + x, SUB, stride=nx)
                tall[tile, spot, :] = value[:, lanes]
                slope[tile, spot, :] = rise[:, lanes]

    for view in range(views):
        for tile in range(ztiles):
            order = ord_ref[view:view + 1, tile * LANES:(tile + 1) * LANES]
            sign = jnp.where(order == 0, -1.0, 1.0)
            sgn_ref[view * ztiles + tile] = jnp.broadcast_to(sign, (SUB, LANES))
    for bump in range(bumps):
        centre = jnp.full((SUB, LANES), cen_ref[bump] * SCALE, jnp.float32)
        factor = jnp.exp2(-centre * centre)
        c2_ref[bump] = 2.0 * centre
        wop_ref[bump] = opa_ref[bump] * factor
        for channel in range(3):
            wcol_ref[channel, bump] = col_ref[channel, bump] * factor

    lane = lax.broadcasted_iota(jnp.int32, (SUB, LANES), 1)
    pairs = ztiles // WIDE

    def render(group, view, first):
        rate = [sgn_ref[view * ztiles + first + a] * LOG2E for a in range(WIDE)]

        def plane(y, carry):
            offset = off_ref[view, iy * ny + y]
            whole = offset >> 2
            frac = (offset & 3).astype(jnp.float32) * 0.25
            spot = pl.ds(pl.multiple_of(y * nx + group * SUB, SUB), SUB)
            turned = []
            for a in range(WIDE + 1):
                mixed = tall[first + a, spot, :] + frac * slope[first + a, spot, :]
                turned.append(pltpu.roll(mixed, (LANES - whole) & (LANES - 1), 1))
            inside = lane < LANES - whole
            result = []
            for a in range(WIDE):
                sums, depth, light = carry[a]
                s = jnp.where(inside, turned[a], turned[a + 1])
                bump = [jnp.exp2(s * (c2_ref[b] - s)) for b in range(bumps)]
                terms = [wop_ref[b] * bump[b] for b in range(bumps)]
                while len(terms) > 1:
                    terms = [i + j for i, j in zip(terms[::2], terms[1::2])]
                depth = depth + terms[0]
                new = jnp.exp2(rate[a] * depth)
                step = new - light
                sums = tuple(sums[b] + step * bump[b] for b in range(bumps))
                result.append((sums, depth, new))
            return tuple(result)

        def several(i, carry):
            for j in range(UNROLL):
                carry = plane(i * UNROLL + j, carry)
            return carry

        zero = jnp.zeros((SUB, LANES), jnp.float32)
        start = tuple(((zero,) * bumps, zero, zero + 1.0) for a in range(WIDE))
        ended = lax.fori_loop(0, ny // UNROLL, several, start)
        for a in range(WIDE):
            sums, depth, light = ended[a]
            sign = sgn_ref[view * ztiles + first + a]
            factor = jnp.where(sign > 0.0, jnp.exp(-depth), -1.0)
            values = []
            for channel in range(3):
                total = wcol_ref[channel, 0] * sums[0]
                for b in range(1, bumps):
                    total += wcol_ref[channel, b] * sums[b]
                values.append(total * factor)
            values.append(depth)
            for j in range(per_group):
                for channel, value in enumerate(values):
                    part[group * per_group + j, view, channel, first + a] = (
                        value[j * rows:(j + 1) * rows])

    def share(owner):
        return pltpu.make_async_remote_copy(
            src_ref=part.at[owner], dst_ref=got.at[iy], send_sem=part_send.at[owner],
            recv_sem=part_recv.at[iy], device_id={"sy": owner}, device_id_type=MESH)

    own_group = iy // per_group

    @pl.loop(0, groups)
    def _(turn):
        group = lax.rem(own_group + 1 + turn, groups)

        @pl.loop(0, views * pairs)
        def _(item):
            render(group, item // pairs, lax.rem(item, pairs) * WIDE)

        for j in range(per_group):
            owner = group * per_group + j

            @pl.when(owner != iy)
            def _():
                share(owner).start()

            @pl.when(owner == iy)
            def _():
                got[iy] = part[iy]

    for other in range(n_y):
        @pl.when(other != iy)
        def _():
            pltpu.make_async_remote_copy(
                src_ref=part.at[other], dst_ref=got.at[other], send_sem=part_send.at[other],
                recv_sem=part_recv.at[other], device_id={"sy": other}, device_id_type=MESH,
            ).wait_recv()

    for view in range(views):
        for tile in range(ztiles):
            lanes = slice(tile * LANES, (tile + 1) * LANES)
            rising = sgn_ref[view * ztiles + tile][:rows] < 0.0
            depths = [got[source, view, 3, tile] for source in range(n_y)]
            total = depths[0]
            for depth in depths[1:]:
                total = total + depth
            front = jnp.zeros_like(total)
            image = [jnp.zeros_like(total)] * 3
            for source in range(n_y):
                before = jnp.where(rising, front, total - front - depths[source])
                seen = jnp.exp(-before)
                image = [image[c] + got[source, view, c, tile] * seen for c in range(3)]
                front = front + depths[source]
            for c in range(3):
                img_ref[view, c, :, lanes] = image[c]
            tr_ref[view, :, lanes] = jnp.exp(-total)

    for other in range(n_y):
        @pl.when(other != iy)
        def _():
            share(other).wait_send()
    out_copy.wait()


def per_device(n_x, n_y, scalar_field, diffusivity, reaction_rate, shear_offsets, depth_order,
               tf_centres, tf_colour, tf_opacity):
    nx, ny, nz = scalar_field.shape
    views, bumps = depth_order.shape[0], tf_centres.shape[0]
    rows, ztiles = nx // n_y, nz // LANES
    f32 = jnp.float32
    vmem = pl.BlockSpec(memory_space=pltpu.VMEM)
    smem = pl.BlockSpec(memory_space=pltpu.SMEM)

    def space(*shape):
        return pltpu.VMEM(shape, f32)

    x_face, y_face = space(ny, nz), space(nx, nz)
    x_faces, y_faces = space(STEPS, ny, nz), space(STEPS, nx, nz)
    shares = space(n_y, views, 4, ztiles, rows, LANES)
    return pl.pallas_call(
        functools.partial(kernel, n_x, n_y),
        out_shape=(
            jax.ShapeDtypeStruct((nx, ny, nz), f32),
            jax.ShapeDtypeStruct((views, 3, rows, nz), f32),
            jax.ShapeDtypeStruct((views, rows, nz), f32),
        ),
        in_specs=[vmem, vmem, vmem, smem, vmem, smem, smem, smem],
        out_specs=(pl.BlockSpec(memory_space=pl.ANY), vmem, vmem),
        scratch_shapes=[
            space(2, nx, ny + SUB, nz), space(nx, ny + SUB, nz),
            x_faces, x_faces, x_face, x_face,
            y_faces, y_faces, y_faces, y_faces,
            y_face, y_face, y_face, y_face, y_face, y_face,
            space(ztiles + 1, ny * nx, LANES), space(ztiles + 1, ny * nx, LANES),
            shares, shares,
            space(views * ztiles, SUB, LANES), space(bumps, SUB, LANES),
            space(bumps, SUB, LANES), space(3, bumps, SUB, LANES),
            pltpu.SemaphoreType.DMA((STEPS + 1, 4)), pltpu.SemaphoreType.DMA((STEPS + 1, 4)),
            pltpu.SemaphoreType.DMA((n_y,)), pltpu.SemaphoreType.DMA((n_y,)),
            pltpu.SemaphoreType.DMA,
        ],
        compiler_params=pltpu.CompilerParams(
            collective_id=0, has_side_effects=True, vmem_limit_bytes=48 * 1024 * 1024),
    )(scalar_field, diffusivity, reaction_rate, shear_offsets, depth_order,
      tf_centres, tf_colour, tf_opacity)


def solution(mesh):
    grid = P("sx", "sy", None)
    return jax.shard_map(
        functools.partial(per_device, mesh.shape["sx"], mesh.shape["sy"]),
        mesh=mesh,
        in_specs=(grid, grid, grid, P(), P(), P(), P(), P()),
        out_specs=(grid, P(None, None, ("sx", "sy"), None), P(None, ("sx", "sy"), None)),
        check_vma=False,
    )
```

profile of v0, /device:TPU:5, one launch (start us, length us, event | category | flops | bytes accessed | tf_op | source)
XLA Modules:
  0.0 119.4 jit_solution(17146936207328318266)
XLA Ops:
  0.6 0.0 copy-start
  0.6 1.6 %copy-done = f32[32,32,512]{2,1,0:T(8,128)S(1)} copy-done((f32[32,32,512]{2,1,0:T(8,128)S(1)}, f32[32,32,512]{2,1,0:T(8,128)}, u32[]{:S(2)}) %copy-start) | copy-done | bytes 2097176
  2.2 0.0 copy-start.1
  2.2 0.7 copy-done.1
  2.9 0.0 copy-start.2
  2.9 0.7 copy-done.2
  3.6 0.0 copy-start.3
  3.6 0.7 copy-done.3
  4.3 0.0 copy-start.4
  4.3 0.7 copy-done.4
  4.9 0.0 copy-start.5
  5.0 0.7 copy-done.5
  5.6 111.2 %shard_map.103 = (f32[32,32,512]{2,1,0:T(8,128)S(1)}, f32[4,3,4,512]{3,2,1,0:T(4,128)S(1)}, f32[4,4,512]{2,1,0:T(4,128)S(1)}) custom-call(f32[32,32,512]{2,1,0:T(8,128)S(1)} %copy-done, f32[32,32,512]{2,1,0:T(8,128)} %d_ref.1, f32[32,32,512]{2,1,0:T(8,128)} %r_ref.1, s32[4,256]{1,0:T(4,128)S(1)} %copy-done.2, s32[4,512]{1,0:T(4,128)S(1)} %copy-done.1, ...), custom_call_target="tpu_custom_call" | custom-call | tf_op jit(solution)/shard_map/pallas_call | solution.py:355
  116.8 1.3 %copy.14 = f32[32,32,512]{2,1,0:T(8,128)} copy(f32[32,32,512]{2,1,0:T(8,128)S(1)} %get-tuple-element.6) | data formatting | bytes 4194304
  118.1 0.6 copy.15
  118.8 0.6 copy.16
Async XLA Ops:
  0.6 1.6 %copy-start = (f32[32,32,512]{2,1,0:T(8,128)S(1)}, f32[32,32,512]{2,1,0:T(8,128)}, u32[]{:S(2)}) copy-start(f32[32,32,512]{2,1,0:T(8,128)} %u_ref.1) | copy-start | bytes 6291460
  2.2 0.7 copy-start.1
  2.9 0.7 copy-start.2
  3.6 0.7 copy-start.3
  4.3 0.7 copy-start.4
  4.9 0.7 copy-start.5
where the time goes:
time: 120 us; the launch traced here: 119 us
  Pallas kernels  111 us (92%)
  local copies, waits for them, and re-layouts  7.53 us (6%)
    pallas_call x1, Pallas kernels, per_device(): pl.pallas_call(functools.partial(kernel, n_x, n_y), out_shape=(jax.ShapeD...  111 us
    unnamed x15, local copies, waits for them, and re-layouts  7.53 us

commit v1 on v0

--- a/solution.py
+++ b/solution.py
@@ -16,7 +16,7 @@
 MESH = pl.DeviceIdType.MESH
 LANES = 128
 SUB = 8
-UNROLL = 2
+UNROLL = 8
 WIDE = 2
 
 
@@ -26,14 +26,14 @@
 
 def kernel(
     n_x, n_y,
-    u_ref, d_ref, r_ref, off_ref, ord_ref, cen_ref, col_ref, opa_ref,
+    u_hbm, d_hbm, r_hbm, off_ref, ord_ref, cen_ref, col_ref, opa_ref,
     f_ref, img_ref, tr_ref,
     field, cond, x_lo, x_hi, dx_lo, dx_hi, p_lo, p_hi, y_lo, y_hi,
     dp_lo, dp_hi, dy_lo, dy_hi, del_lo, del_hi, tall, slope,
     part, got, sgn_ref, c2_ref, wop_ref, wcol_ref,
-    halo_send, halo_recv, part_send, part_recv, out_sem,
+    d_ref, r_ref, halo_send, halo_recv, part_send, part_recv, out_sem, in_sem,
 ):
-    nx, ny, nz = u_ref.shape
+    nx, ny, nz = u_hbm.shape
     views = ord_ref.shape[0]
     bumps = cen_ref.shape[0]
     ztiles = nz // LANES
@@ -41,6 +41,13 @@
     per_group = SUB // rows
     groups = nx // SUB
     ix, iy = lax.axis_index("sx"), lax.axis_index("sy")
+
+    fetches = [
+        pltpu.make_async_copy(src, dst, in_sem.at[i]) for i, (src, dst) in enumerate((
+            (u_hbm, field.at[0, :, pl.ds(0, ny)]), (d_hbm, d_ref), (r_hbm, r_ref)))
+    ]
+    for fetch in fetches:
+        fetch.start()
 
     barrier = pltpu.get_barrier_semaphore()
     for hop in range(1, n_y):
@@ -104,24 +111,19 @@
             landings[side][...] = jnp.zeros_like(landings[side])
             diff_landings[side][...] = jnp.zeros_like(diff_landings[side])
 
+    fetches[0].wait()
+    fetches[1].wait()
+
     @pl.loop(0, groups)
     def _(block):
         base = pl.multiple_of(block * SUB, SUB)
         for ref, row, out in (
-            (u_ref, 0, p_lo.at[0]), (u_ref, ny - 1, p_hi.at[0]),
+            (field.at[0], 0, p_lo.at[0]), (field.at[0], ny - 1, p_hi.at[0]),
             (d_ref, 0, dp_lo), (d_ref, ny - 1, dp_hi),
         ):
             out[pl.ds(base, SUB), :] = jnp.concatenate(
                 [ref[base + j, row:row + 1, :] for j in range(SUB)], axis=0)
 
-    @pl.loop(0, nx)
-    def _(x):
-        for t in range(ny // SUB):
-            cut = pl.ds(t * SUB, SUB)
-            now = u_ref[x, cut, :]
-            field[0, x, cut, :] = now
-            cond[x, cut, :] = conduct(d_ref[x, cut, :], now)
-
     arrivals = (n_y - 1) + (ix > 0).astype(jnp.int32) + (ix < n_x - 1).astype(jnp.int32)
     pl.semaphore_wait(barrier, arrivals)
     start_halos(0)
@@ -132,14 +134,17 @@
 
     for step in range(STEPS):
         now, later = step % 2, (step + 1) % 2
-        if step:
-            @pl.loop(0, nx)
-            def _(x):
-                for t in range(ny // SUB):
-                    cut = pl.ds(t * SUB, SUB)
-                    cond[x, cut, :] = conduct(d_ref[x, cut, :], field[now, x, cut, :])
-
-        @pl.loop(0, nx)
+
+        @pl.loop(0, nx, unroll=4)
+        def _(x):
+            for t in range(ny // SUB):
+                cut = pl.ds(t * SUB, SUB)
+                cond[x, cut, :] = conduct(d_ref[x, cut, :], field[now, x, cut, :])
+
+        if step == 0:
+            fetches[2].wait()
+
+        @pl.loop(0, nx, unroll=2)
         def _(x):
             below, above = jnp.maximum(x - 1, 0), jnp.minimum(x + 1, nx - 1)
             carried = None
@@ -198,7 +203,7 @@
     for ref in (tall, slope):
         ref[ztiles] = jnp.zeros_like(ref[ztiles])
 
-    @pl.loop(0, nx)
+    @pl.loop(0, nx, unroll=2)
     def _(x):
         for t in range(ny // SUB):
             value = field[last, x, pl.ds(t * SUB, SUB), :] * SCALE
@@ -344,6 +349,7 @@
     rows, ztiles = nx // n_y, nz // LANES
     f32 = jnp.float32
     vmem = pl.BlockSpec(memory_space=pltpu.VMEM)
+    far = pl.BlockSpec(memory_space=pl.ANY)
     smem = pl.BlockSpec(memory_space=pltpu.SMEM)
 
     def space(*shape):
@@ -359,8 +365,8 @@
             jax.ShapeDtypeStruct((views, 3, rows, nz), f32),
             jax.ShapeDtypeStruct((views, rows, nz), f32),
         ),
-        in_specs=[vmem, vmem, vmem, smem, vmem, smem, smem, smem],
-        out_specs=(pl.BlockSpec(memory_space=pl.ANY), vmem, vmem),
+        in_specs=[far, far, far, smem, vmem, smem, smem, smem],
+        out_specs=(far, vmem, vmem),
         scratch_shapes=[
             space(2, nx, ny + SUB, nz), space(nx, ny + SUB, nz),
             x_faces, x_faces, x_face, x_face,
@@ -370,12 +376,13 @@
             shares, shares,
             space(views * ztiles, SUB, LANES), space(bumps, SUB, LANES),
             space(bumps, SUB, LANES), space(3, bumps, SUB, LANES),
+            space(nx, ny, nz), space(nx, ny, nz),
             pltpu.SemaphoreType.DMA((STEPS + 1, 4)), pltpu.SemaphoreType.DMA((STEPS + 1, 4)),
             pltpu.SemaphoreType.DMA((n_y,)), pltpu.SemaphoreType.DMA((n_y,)),
-            pltpu.SemaphoreType.DMA,
+            pltpu.SemaphoreType.DMA, pltpu.SemaphoreType.DMA((3,)),
         ],
         compiler_params=pltpu.CompilerParams(
-            collective_id=0, has_side_effects=True, vmem_limit_bytes=48 * 1024 * 1024),
+            collective_id=0, has_side_effects=True, vmem_limit_bytes=60 * 1024 * 1024),
     )(scalar_field, diffusivity, reaction_rate, shear_offsets, depth_order,
       tf_centres, tf_colour, tf_opacity)
 

time: 120 us -> 73.9 us (0.62)
  Pallas kernels: 111 us -> 68.5 us
  local copies, waits for them, and re-layouts: 7.53 us -> 4.48 us
    pallas_call x1, Pallas kernels: 111 us -> 68.5 us  [per_device(): pl.pallas_call(functools.partial(kernel, n_x, n_y), out_shape=(jax.ShapeD...]
    unnamed x15 -> x7, local copies, waits for them, and re-layouts: 7.53 us -> 4.48 us
where the time goes in v1:
time: 73.9 us; the launch traced here: 73.7 us
  Pallas kernels  68.5 us (93%)
  local copies, waits for them, and re-layouts  4.48 us (6%)
    pallas_call x1, Pallas kernels, per_device(): pl.pallas_call(functools.partial(kernel, n_x, n_y), out_shape=(jax.ShapeD...  68.5 us
    unnamed x7, local copies, waits for them, and re-layouts  4.48 us

profile of v1, /device:TPU:5, one launch (start us, length us, event | category | flops | bytes accessed | tf_op | source)
XLA Modules:
  0.0 73.7 jit_solution(18137025676551974510)
XLA Ops:
  0.6 68.5 %shard_map.103 = (f32[32,32,512]{2,1,0:T(8,128)}, f32[4,3,4,512]{3,2,1,0:T(4,128)}, f32[4,4,512]{2,1,0:T(4,128)}) custom-call(f32[32,32,512]{2,1,0:T(8,128)} %u_hbm.1, f32[32,32,512]{2,1,0:T(8,128)} %d_hbm.1, f32[32,32,512]{2,1,0:T(8,128)} %r_hbm.1, s32[4,256]{1,0:T(4,128)} %off_ref.1, s32[4,512]{1,0:T(4,128)} %ord_ref.1, f32[8]{0:T(128)} %cen_ref.1, ...), custom_call_target="tpu_custom_call" | custom-call | tf_op jit(solution)/shard_map/pallas_call | solution.py:361
  69.2 0.0 copy-start
  69.2 0.0 copy-start.1
  69.2 3.2 %copy.14 = f32[32,32,512]{2,1,0:T(8,128)} copy(f32[32,32,512]{2,1,0:T(8,128)} %get-tuple-element.6) | data formatting | bytes 4194304
  72.4 0.0 copy-done
  72.4 0.6 copy.15
  73.1 0.0 copy-done.1
  73.1 0.6 copy.16
Async XLA Ops:
  69.2 3.2 %copy-start = (f32[4,3,4,512]{3,2,1,0:T(4,128)S(1)}, f32[4,3,4,512]{3,2,1,0:T(4,128)}, u32[]{:S(2)}) copy-start(f32[4,3,4,512]{3,2,1,0:T(4,128)} %get-tuple-element.7) | copy-start | bytes 294916
  69.2 3.9 %copy-start.1 = (f32[4,4,512]{2,1,0:T(4,128)S(1)}, f32[4,4,512]{2,1,0:T(4,128)}, u32[]{:S(2)}) copy-start(f32[4,4,512]{2,1,0:T(4,128)} %get-tuple-element.8) | copy-start | bytes 98308

commit v2 on v1

--- a/solution.py
+++ b/solution.py
@@ -16,7 +16,7 @@
 MESH = pl.DeviceIdType.MESH
 LANES = 128
 SUB = 8
-UNROLL = 8
+UNROLL = 16
 WIDE = 2
 
 
@@ -26,12 +26,14 @@
 
 def kernel(
     n_x, n_y,
-    u_hbm, d_hbm, r_hbm, off_ref, ord_ref, cen_ref, col_ref, opa_ref,
+    u_hbm, d_hbm, r_hbm, off_hbm, ord_hbm, cen_hbm, col_hbm, opa_hbm,
     f_ref, img_ref, tr_ref,
     field, cond, x_lo, x_hi, dx_lo, dx_hi, p_lo, p_hi, y_lo, y_hi,
     dp_lo, dp_hi, dy_lo, dy_hi, del_lo, del_hi, tall, slope,
-    part, got, sgn_ref, c2_ref, wop_ref, wcol_ref,
-    d_ref, r_ref, halo_send, halo_recv, part_send, part_recv, out_sem, in_sem,
+    part, mate, both, got, sgn_ref, c2_ref, wop_ref, wcol_ref,
+    d_ref, r_ref, off_ref, ord_ref, cen_ref, col_ref, opa_ref,
+    halo_send, halo_recv, mate_send, mate_recv, part_send, part_recv,
+    out_sem, in_sem,
 ):
     nx, ny, nz = u_hbm.shape
     views = ord_ref.shape[0]
@@ -44,7 +46,9 @@
 
     fetches = [
         pltpu.make_async_copy(src, dst, in_sem.at[i]) for i, (src, dst) in enumerate((
-            (u_hbm, field.at[0, :, pl.ds(0, ny)]), (d_hbm, d_ref), (r_hbm, r_ref)))
+            (u_hbm, field.at[0, :, pl.ds(0, ny)]), (d_hbm, d_ref), (r_hbm, r_ref),
+            (off_hbm, off_ref), (ord_hbm, ord_ref), (cen_hbm, cen_ref), (col_hbm, col_ref),
+            (opa_hbm, opa_ref)))
     ]
     for fetch in fetches:
         fetch.start()
@@ -114,7 +118,7 @@
     fetches[0].wait()
     fetches[1].wait()
 
-    @pl.loop(0, groups)
+    @pl.loop(0, groups, unroll=True)
     def _(block):
         base = pl.multiple_of(block * SUB, SUB)
         for ref, row, out in (
@@ -135,7 +139,7 @@
     for step in range(STEPS):
         now, later = step % 2, (step + 1) % 2
 
-        @pl.loop(0, nx, unroll=4)
+        @pl.loop(0, nx, unroll=8)
         def _(x):
             for t in range(ny // SUB):
                 cut = pl.ds(t * SUB, SUB)
@@ -144,17 +148,27 @@
         if step == 0:
             fetches[2].wait()
 
-        @pl.loop(0, nx, unroll=2)
+        @pl.loop(0, nx, unroll=4)
         def _(x):
             below, above = jnp.maximum(x - 1, 0), jnp.minimum(x + 1, nx - 1)
+            tiles = ny // SUB
+            cuts = [pl.ds(t * SUB, SUB) for t in range(tiles)]
+            us = [field[now, x, cut, :] for cut in cuts]
+            ks = [cond[x, cut, :] for cut in cuts]
+            up_u = [pltpu.roll(u, SUB - 1, 0) for u in us]
+            up_k = [pltpu.roll(k, SUB - 1, 0) for k in ks]
             carried = None
-            for t in range(ny // SUB):
-                cut, shifted = pl.ds(t * SUB, SUB), pl.ds(t * SUB + 1, SUB)
-                u, k = field[now, x, cut, :], cond[x, cut, :]
+            for t, cut in enumerate(cuts):
+                u, k = us[t], ks[t]
                 change = (k + cond[below, cut, :]) * (field[now, below, cut, :] - u)
                 change += (k + cond[above, cut, :]) * (field[now, above, cut, :] - u)
-                flux = (k + cond[x, shifted, :]) * (field[now, x, shifted, :] - u)
-                if t == ny // SUB - 1:
+                if t < tiles - 1:
+                    next_u = jnp.where(row_at == SUB - 1, up_u[t + 1], up_u[t])
+                    next_k = jnp.where(row_at == SUB - 1, up_k[t + 1], up_k[t])
+                else:
+                    next_u, next_k = up_u[t], up_k[t]
+                flux = (k + next_k) * (next_u - u)
+                if t == tiles - 1:
                     flux = jnp.where(row_at == SUB - 1, 0.0, flux)
                 turned = pltpu.roll(flux, 1, 0)
                 change += flux - jnp.where(row_at == 0, 0.0 if t == 0 else carried, turned)
@@ -180,7 +194,7 @@
             u, beside = packed[step], land[step]
             out[...] = 0.5 * (conduct(own[...], u) + conduct(diff[...], beside)) * (beside - u)
 
-        @pl.loop(0, groups)
+        @pl.loop(0, groups, unroll=True)
         def _(block):
             base = pl.multiple_of(block * SUB, SUB)
             for packed, delta, row in ((p_lo, del_lo, 0), (p_hi, del_hi, ny - 1)):
@@ -214,6 +228,8 @@
                 tall[tile, spot, :] = value[:, lanes]
                 slope[tile, spot, :] = rise[:, lanes]
 
+    for fetch in fetches[3:]:
+        fetch.wait()
     for view in range(views):
         for tile in range(ztiles):
             order = ord_ref[view:view + 1, tile * LANES:(tile + 1) * LANES]
@@ -282,51 +298,86 @@
                     part[group * per_group + j, view, channel, first + a] = (
                         value[j * rows:(j + 1) * rows])
 
-    def share(owner):
+    core, pair = lax.rem(iy, 2), iy // 2
+    twin = iy + 1 - 2 * core
+    group_pairs = per_group // 2
+    flip = (1 - 2 * core).astype(jnp.float32)
+
+    def hand(which):
         return pltpu.make_async_remote_copy(
-            src_ref=part.at[owner], dst_ref=got.at[iy], send_sem=part_send.at[owner],
-            recv_sem=part_recv.at[iy], device_id={"sy": owner}, device_id_type=MESH)
+            src_ref=part.at[2 * which + 1 - core], dst_ref=mate.at[which],
+            send_sem=mate_send.at[which], recv_sem=mate_recv.at[which],
+            device_id={"sy": twin}, device_id_type=MESH)
+
+    def share(which, slot):
+        return pltpu.make_async_remote_copy(
+            src_ref=both.at[which], dst_ref=got.at[slot], send_sem=part_send.at[which],
+            recv_sem=part_recv.at[slot], device_id={"sy": 2 * which + core}, device_id_type=MESH)
+
+    def merge(which):
+        hand(which).wait_recv()
+        for view in range(views):
+            for tile in range(ztiles):
+                mine_first = sgn_ref[view * ztiles + tile][:rows] * flip < 0.0
+                mine = [part[2 * which + core, view, c, tile] for c in range(4)]
+                other = [mate[which, view, c, tile] for c in range(4)]
+                dim = jnp.exp(-jnp.where(mine_first, mine[3], other[3]))
+                for c in range(3):
+                    near = jnp.where(mine_first, mine[c], other[c])
+                    far = jnp.where(mine_first, other[c], mine[c])
+                    both[which, view, c, tile] = near + dim * far
+                both[which, view, 3, tile] = mine[3] + other[3]
+
+    def finish(group):
+        for j in range(group_pairs):
+            which = group * group_pairs + j
+            merge(which)
+
+            @pl.when(which != pair)
+            def _():
+                share(which, pair).start()
+
+            @pl.when(which == pair)
+            def _():
+                got[pair] = both[pair]
 
     own_group = iy // per_group
+    early = min(2, views * pairs)
 
     @pl.loop(0, groups)
     def _(turn):
         group = lax.rem(own_group + 1 + turn, groups)
 
-        @pl.loop(0, views * pairs)
-        def _(item):
+        def item_at(item):
             render(group, item // pairs, lax.rem(item, pairs) * WIDE)
 
-        for j in range(per_group):
-            owner = group * per_group + j
-
-            @pl.when(owner != iy)
-            def _():
-                share(owner).start()
-
-            @pl.when(owner == iy)
-            def _():
-                got[iy] = part[iy]
-
-    for other in range(n_y):
-        @pl.when(other != iy)
+        pl.loop(0, early)(item_at)
+
+        @pl.when(turn > 0)
         def _():
-            pltpu.make_async_remote_copy(
-                src_ref=part.at[other], dst_ref=got.at[other], send_sem=part_send.at[other],
-                recv_sem=part_recv.at[other], device_id={"sy": other}, device_id_type=MESH,
-            ).wait_recv()
+            finish(lax.rem(own_group + turn, groups))
+
+        pl.loop(early, views * pairs)(item_at)
+        for j in range(group_pairs):
+            hand(group * group_pairs + j).start()
+
+    finish(own_group)
+    for other in range(n_y // 2):
+        @pl.when(other != pair)
+        def _():
+            share(other, other).wait_recv()
 
     for view in range(views):
         for tile in range(ztiles):
             lanes = slice(tile * LANES, (tile + 1) * LANES)
             rising = sgn_ref[view * ztiles + tile][:rows] < 0.0
-            depths = [got[source, view, 3, tile] for source in range(n_y)]
+            depths = [got[source, view, 3, tile] for source in range(n_y // 2)]
             total = depths[0]
             for depth in depths[1:]:
                 total = total + depth
             front = jnp.zeros_like(total)
             image = [jnp.zeros_like(total)] * 3
-            for source in range(n_y):
+            for source in range(n_y // 2):
                 before = jnp.where(rising, front, total - front - depths[source])
                 seen = jnp.exp(-before)
                 image = [image[c] + got[source, view, c, tile] * seen for c in range(3)]
@@ -335,10 +386,12 @@
                 img_ref[view, c, :, lanes] = image[c]
             tr_ref[view, :, lanes] = jnp.exp(-total)
 
-    for other in range(n_y):
-        @pl.when(other != iy)
+    for other in range(n_y // 2):
+        hand(other).wait_send()
+
+        @pl.when(other != pair)
         def _():
-            share(other).wait_send()
+            share(other, pair).wait_send()
     out_copy.wait()
 
 
@@ -350,7 +403,7 @@
     f32 = jnp.float32
     vmem = pl.BlockSpec(memory_space=pltpu.VMEM)
     far = pl.BlockSpec(memory_space=pl.ANY)
-    smem = pl.BlockSpec(memory_space=pltpu.SMEM)
+    pinned = pl.BlockSpec(memory_space=pltpu.HBM)
 
     def space(*shape):
         return pltpu.VMEM(shape, f32)
@@ -358,6 +411,7 @@
     x_face, y_face = space(ny, nz), space(nx, nz)
     x_faces, y_faces = space(STEPS, ny, nz), space(STEPS, nx, nz)
     shares = space(n_y, views, 4, ztiles, rows, LANES)
+    halves = space(n_y // 2, views, 4, ztiles, rows, LANES)
     return pl.pallas_call(
         functools.partial(kernel, n_x, n_y),
         out_shape=(
@@ -365,7 +419,7 @@
             jax.ShapeDtypeStruct((views, 3, rows, nz), f32),
             jax.ShapeDtypeStruct((views, rows, nz), f32),
         ),
-        in_specs=[far, far, far, smem, vmem, smem, smem, smem],
+        in_specs=[pinned] * 8,
         out_specs=(far, vmem, vmem),
         scratch_shapes=[
             space(2, nx, ny + SUB, nz), space(nx, ny + SUB, nz),
@@ -373,13 +427,16 @@
             y_faces, y_faces, y_faces, y_faces,
             y_face, y_face, y_face, y_face, y_face, y_face,
             space(ztiles + 1, ny * nx, LANES), space(ztiles + 1, ny * nx, LANES),
-            shares, shares,
+            shares, halves, halves, halves,
             space(views * ztiles, SUB, LANES), space(bumps, SUB, LANES),
             space(bumps, SUB, LANES), space(3, bumps, SUB, LANES),
             space(nx, ny, nz), space(nx, ny, nz),
+            pltpu.SMEM(shear_offsets.shape, jnp.int32), pltpu.VMEM(depth_order.shape, jnp.int32),
+            pltpu.SMEM(tf_centres.shape, f32), pltpu.SMEM(tf_colour.shape, f32),
+            pltpu.SMEM(tf_opacity.shape, f32),
             pltpu.SemaphoreType.DMA((STEPS + 1, 4)), pltpu.SemaphoreType.DMA((STEPS + 1, 4)),
-            pltpu.SemaphoreType.DMA((n_y,)), pltpu.SemaphoreType.DMA((n_y,)),
-            pltpu.SemaphoreType.DMA, pltpu.SemaphoreType.DMA((3,)),
+            *[pltpu.SemaphoreType.DMA((n_y // 2,))] * 4,
+            pltpu.SemaphoreType.DMA, pltpu.SemaphoreType.DMA((8,)),
         ],
         compiler_params=pltpu.CompilerParams(
             collective_id=0, has_side_effects=True, vmem_limit_bytes=60 * 1024 * 1024),

time: 73.9 us -> 63 us (0.85)
  Pallas kernels: 68.5 us -> 57.7 us
    pallas_call x1, Pallas kernels: 68.5 us -> 57.7 us  [per_device(): pl.pallas_call(functools.partial(kernel, n_x, n_y), out_shape=(jax.ShapeD...]
where the time goes in v2:
time: 63 us; the launch traced here: 62.9 us
  Pallas kernels  57.7 us (92%)
  local copies, waits for them, and re-layouts  4.48 us (7%)
  between operations  0.66 us (1%)
    pallas_call x1, Pallas kernels, per_device(): pl.pallas_call(functools.partial(kernel, n_x, n_y), out_shape=(jax.ShapeD...  57.7 us
    unnamed x7, local copies, waits for them, and re-layouts  4.48 us

profile of v2, /device:TPU:5, one launch (start us, length us, event | category | flops | bytes accessed | tf_op | source)
XLA Modules:
  0.0 62.9 jit_solution(17059128653692421290)
XLA Ops:
  0.6 57.7 %shard_map.103 = (f32[32,32,512]{2,1,0:T(8,128)}, f32[4,3,4,512]{3,2,1,0:T(4,128)}, f32[4,4,512]{2,1,0:T(4,128)}) custom-call(f32[32,32,512]{2,1,0:T(8,128)} %u_hbm.1, f32[32,32,512]{2,1,0:T(8,128)} %d_hbm.1, f32[32,32,512]{2,1,0:T(8,128)} %r_hbm.1, s32[4,256]{1,0:T(4,128)} %off_hbm.1, s32[4,512]{1,0:T(4,128)} %ord_hbm.1, f32[8]{0:T(128)} %cen_hbm.1, ...), custom_call_target="tpu_custom_call" | custom-call | tf_op jit(solution)/shard_map/pallas_call | solution.py:415
  58.4 0.0 copy-start
  58.4 0.0 copy-start.1
  58.4 3.2 %copy.14 = f32[32,32,512]{2,1,0:T(8,128)} copy(f32[32,32,512]{2,1,0:T(8,128)} %get-tuple-element.6) | data formatting | bytes 4194304
  61.6 0.0 copy-done
  61.6 0.6 %copy.15 = f32[4,3,4,512]{3,2,1,0:T(4,128)} copy(f32[4,3,4,512]{3,2,1,0:T(4,128)S(1)} %copy-done) | data formatting | bytes 196608
  62.3 0.0 copy-done.1
  62.3 0.6 copy.16
Async XLA Ops:
  58.4 3.2 %copy-start = (f32[4,3,4,512]{3,2,1,0:T(4,128)S(1)}, f32[4,3,4,512]{3,2,1,0:T(4,128)}, u32[]{:S(2)}) copy-start(f32[4,3,4,512]{3,2,1,0:T(4,128)} %get-tuple-element.7) | copy-start | bytes 294916
  58.4 3.9 %copy-start.1 = (f32[4,4,512]{2,1,0:T(4,128)S(1)}, f32[4,4,512]{2,1,0:T(4,128)}, u32[]{:S(2)}) copy-start(f32[4,4,512]{2,1,0:T(4,128)} %get-tuple-element.8) | copy-start | bytes 98308

commit v3 on v2

--- a/solution.py
+++ b/solution.py
@@ -16,7 +16,8 @@
 MESH = pl.DeviceIdType.MESH
 LANES = 128
 SUB = 8
-UNROLL = 16
+UNROLL = 32
+CHUNKS = 8
 WIDE = 2
 
 
@@ -221,12 +222,20 @@
     def _(x):
         for t in range(ny // SUB):
             value = field[last, x, pl.ds(t * SUB, SUB), :] * SCALE
-            rise = jnp.where(col_at == nz - 1, 0.0, pltpu.roll(value, nz - 1, 1)) - value
             for tile in range(ztiles):
-                lanes = slice(tile * LANES, (tile + 1) * LANES)
                 spot = pl.ds(t * SUB * nx + x, SUB, stride=nx)
-                tall[tile, spot, :] = value[:, lanes]
-                slope[tile, spot, :] = rise[:, lanes]
+                tall[tile, spot, :] = value[:, tile * LANES:(tile + 1) * LANES]
+
+    lane = lax.broadcasted_iota(jnp.int32, (SUB, LANES), 1)
+
+    @pl.loop(0, ny * nx // SUB, unroll=4)
+    def _(block):
+        spot = pl.ds(pl.multiple_of(block * SUB, SUB), SUB)
+        values = [tall[tile, spot, :] for tile in range(ztiles)]
+        ahead = [pltpu.roll(value, LANES - 1, 1) for value in values] + [0.0]
+        for tile in range(ztiles):
+            beside = jnp.where(lane == LANES - 1, ahead[tile + 1], ahead[tile])
+            slope[tile, spot, :] = beside - values[tile]
 
     for fetch in fetches[3:]:
         fetch.wait()
@@ -243,7 +252,6 @@
         for channel in range(3):
             wcol_ref[channel, bump] = col_ref[channel, bump] * factor
 
-    lane = lax.broadcasted_iota(jnp.int32, (SUB, LANES), 1)
     pairs = ztiles // WIDE
 
     def render(group, view, first):
@@ -274,14 +282,16 @@
                 result.append((sums, depth, new))
             return tuple(result)
 
+        unroll = min(UNROLL, ny)
+
         def several(i, carry):
-            for j in range(UNROLL):
-                carry = plane(i * UNROLL + j, carry)
+            for j in range(unroll):
+                carry = plane(i * unroll + j, carry)
             return carry
 
         zero = jnp.zeros((SUB, LANES), jnp.float32)
         start = tuple(((zero,) * bumps, zero, zero + 1.0) for a in range(WIDE))
-        ended = lax.fori_loop(0, ny // UNROLL, several, start)
+        ended = lax.fori_loop(0, ny // unroll, several, start)
         for a in range(WIDE):
             sums, depth, light = ended[a]
             sign = sgn_ref[view * ztiles + first + a]
@@ -395,6 +405,22 @@
     out_copy.wait()
 
 
+def deliver(*refs):
+    count = (len(refs) - 1) // 2
+    sem = refs[-1]
+    copies = []
+    for src, dst in zip(refs[:count], refs[count:-1]):
+        pieces = CHUNKS if src.shape[0] % CHUNKS == 0 else 1
+        size = src.shape[0] // pieces
+        for piece in range(pieces):
+            cut = pl.ds(piece * size, size)
+            copies.append(pltpu.make_async_copy(src.at[cut], dst.at[cut], sem.at[len(copies)]))
+    for copy in copies:
+        copy.start()
+    for copy in copies:
+        copy.wait()
+
+
 def per_device(n_x, n_y, scalar_field, diffusivity, reaction_rate, shear_offsets, depth_order,
                tf_centres, tf_colour, tf_opacity):
     nx, ny, nz = scalar_field.shape
@@ -412,13 +438,14 @@
     x_faces, y_faces = space(STEPS, ny, nz), space(STEPS, nx, nz)
     shares = space(n_y, views, 4, ztiles, rows, LANES)
     halves = space(n_y // 2, views, 4, ztiles, rows, LANES)
-    return pl.pallas_call(
+    results = (
+        jax.ShapeDtypeStruct((nx, ny, nz), f32),
+        jax.ShapeDtypeStruct((views, 3, rows, nz), f32),
+        jax.ShapeDtypeStruct((views, rows, nz), f32),
+    )
+    made = pl.pallas_call(
         functools.partial(kernel, n_x, n_y),
-        out_shape=(
-            jax.ShapeDtypeStruct((nx, ny, nz), f32),
-            jax.ShapeDtypeStruct((views, 3, rows, nz), f32),
-            jax.ShapeDtypeStruct((views, rows, nz), f32),
-        ),
+        out_shape=results,
         in_specs=[pinned] * 8,
         out_specs=(far, vmem, vmem),
         scratch_shapes=[
@@ -442,6 +469,14 @@
             collective_id=0, has_side_effects=True, vmem_limit_bytes=60 * 1024 * 1024),
     )(scalar_field, diffusivity, reaction_rate, shear_offsets, depth_order,
       tf_centres, tf_colour, tf_opacity)
+    return pl.pallas_call(
+        deliver,
+        out_shape=results,
+        in_specs=[far] * 3,
+        out_specs=(far,) * 3,
+        scratch_shapes=[pltpu.SemaphoreType.DMA((3 * CHUNKS,))],
+        compiler_params=pltpu.CompilerParams(vmem_limit_bytes=60 * 1024 * 1024),
+    )(*made)
 
 
 def solution(mesh):

time: 63 us -> 126 us (2.00)
  Pallas kernels: 57.7 us -> 125 us
  local copies, waits for them, and re-layouts: 4.48 us -> 0 us
    pallas_call x1 -> x2, Pallas kernels: 57.7 us -> 125 us  [the longest x1 68.8 us: per_device(): pl.pallas_call(deliver, out_shape=results, in_specs=[far] * 3, out_specs=...]
    unnamed x7 -> x0, local copies, waits for them, and re-layouts: 4.48 us -> none
where the time goes in v3:
time: 126 us
  Pallas kernels  125 us (99%)
    pallas_call x1, Pallas kernels, per_device(): pl.pallas_call(deliver, out_shape=results, in_specs=[far] * 3, out_specs=...  68.8 us
    pallas_call x1, Pallas kernels, per_device(): pl.pallas_call(functools.partial(kernel, n_x, n_y), out_shape=results, in...  56 us

profile of v3, /device:TPU:5, one launch (start us, length us, event | category | flops | bytes accessed | tf_op | source)
XLA Modules:
  0.0 125.5 jit_solution(10557246787914913597)
XLA Ops:
  0.6 56.0 %shard_map.103 = (f32[32,32,512]{2,1,0:T(8,128)}, f32[4,3,4,512]{3,2,1,0:T(4,128)}, f32[4,4,512]{2,1,0:T(4,128)}) custom-call(f32[32,32,512]{2,1,0:T(8,128)} %u_hbm.1, f32[32,32,512]{2,1,0:T(8,128)} %d_hbm.1, f32[32,32,512]{2,1,0:T(8,128)} %r_hbm.1, s32[4,256]{1,0:T(4,128)} %off_hbm.1, s32[4,512]{1,0:T(4,128)} %ord_hbm.1, f32[8]{0:T(128)} %cen_hbm.1, ...), custom_call_target="tpu_custom_call" | custom-call | tf_op jit(solution)/shard_map/pallas_call | solution.py:446
  56.7 68.8 %shard_map.104 = (f32[32,32,512]{2,1,0:T(8,128)}, f32[4,3,4,512]{3,2,1,0:T(4,128)}, f32[4,4,512]{2,1,0:T(4,128)}) custom-call(f32[32,32,512]{2,1,0:T(8,128)} %get-tuple-element.6.refs_0_, f32[4,3,4,512]{3,2,1,0:T(4,128)} %get-tuple-element.7.refs_1_, f32[4,4,512]{2,1,0:T(4,128)} %get-tuple-element.8.refs_2_), custom_call_target="tpu_custom_call" | custom-call | tf_op jit(solution)/shard_map/pallas_call | solution.py:472

commit v4 on v3

--- a/solution.py
+++ b/solution.py
@@ -134,8 +134,9 @@
     start_halos(0)
     start_halos(STEPS)
 
-    row_at = lax.broadcasted_iota(jnp.int32, (SUB, nz), 0)
-    col_at = lax.broadcasted_iota(jnp.int32, (SUB, nz), 1)
+    row_at = lax.broadcasted_iota(jnp.int32, (SUB, LANES), 0)
+    lane = lax.broadcasted_iota(jnp.int32, (SUB, LANES), 1)
+    first_row, last_row, first_lane = row_at == 0, row_at == SUB - 1, lane == 0
 
     for step in range(STEPS):
         now, later = step % 2, (step + 1) % 2
@@ -153,32 +154,46 @@
         def _(x):
             below, above = jnp.maximum(x - 1, 0), jnp.minimum(x + 1, nx - 1)
             tiles = ny // SUB
-            cuts = [pl.ds(t * SUB, SUB) for t in range(tiles)]
-            us = [field[now, x, cut, :] for cut in cuts]
-            ks = [cond[x, cut, :] for cut in cuts]
-            up_u = [pltpu.roll(u, SUB - 1, 0) for u in us]
-            up_k = [pltpu.roll(k, SUB - 1, 0) for k in ks]
-            carried = None
-            for t, cut in enumerate(cuts):
-                u, k = us[t], ks[t]
-                change = (k + cond[below, cut, :]) * (field[now, below, cut, :] - u)
-                change += (k + cond[above, cut, :]) * (field[now, above, cut, :] - u)
-                if t < tiles - 1:
-                    next_u = jnp.where(row_at == SUB - 1, up_u[t + 1], up_u[t])
-                    next_k = jnp.where(row_at == SUB - 1, up_k[t + 1], up_k[t])
-                else:
-                    next_u, next_k = up_u[t], up_k[t]
-                flux = (k + next_k) * (next_u - u)
-                if t == tiles - 1:
-                    flux = jnp.where(row_at == SUB - 1, 0.0, flux)
-                turned = pltpu.roll(flux, 1, 0)
-                change += flux - jnp.where(row_at == 0, 0.0 if t == 0 else carried, turned)
-                carried = turned
-                ku = k * u
-                right_u, right_k = pltpu.roll(u, nz - 1, 1), pltpu.roll(k, nz - 1, 1)
-                flux = jnp.where(col_at == nz - 1, -ku, (k + right_k) * (right_u - u))
-                change += flux - jnp.where(col_at == 0, ku, pltpu.roll(flux, 1, 1))
-                field[later, x, cut, :] = u + 0.5 * change + r_ref[x, cut, :] * jnp.tanh(u)
+            before = [None] * tiles
+            for tile in range(ztiles):
+                lanes = slice(tile * LANES, (tile + 1) * LANES)
+                rear = slice((tile + 1) * LANES, (tile + 2) * LANES)
+                up_u, up_k, carried = None, None, None
+                for t in range(tiles):
+                    cut = pl.ds(t * SUB, SUB)
+                    u, k = field[now, x, cut, lanes], cond[x, cut, lanes]
+                    change = (k + cond[below, cut, lanes]) * (field[now, below, cut, lanes] - u)
+                    change += (k + cond[above, cut, lanes]) * (field[now, above, cut, lanes] - u)
+
+                    if t == 0:
+                        up_u, up_k = pltpu.roll(u, SUB - 1, 0), pltpu.roll(k, SUB - 1, 0)
+                    if t < tiles - 1:
+                        cut_on = pl.ds((t + 1) * SUB, SUB)
+                        on_u = pltpu.roll(field[now, x, cut_on, lanes], SUB - 1, 0)
+                        on_k = pltpu.roll(cond[x, cut_on, lanes], SUB - 1, 0)
+                        flux = (k + jnp.where(last_row, on_k, up_k)) * (
+                            jnp.where(last_row, on_u, up_u) - u)
+                        up_u, up_k = on_u, on_k
+                    else:
+                        flux = jnp.where(last_row, 0.0, (k + up_k) * (up_u - u))
+                    turned = pltpu.roll(flux, 1, 0)
+                    change += flux - jnp.where(first_row, 0.0 if t == 0 else carried, turned)
+                    carried = turned
+
+                    if tile < ztiles - 1:
+                        on_u, on_k = field[now, x, cut, rear], cond[x, cut, rear]
+                        next_u = pltpu.roll(jnp.where(first_lane, on_u, u), LANES - 1, 1)
+                        next_k = pltpu.roll(jnp.where(first_lane, on_k, k), LANES - 1, 1)
+                    else:
+                        next_u = pltpu.roll(jnp.where(first_lane, 0.0, u), LANES - 1, 1)
+                        next_k = pltpu.roll(jnp.where(first_lane, 0.0, k), LANES - 1, 1)
+                    flux = (k + next_k) * (next_u - u)
+                    turned = pltpu.roll(flux, 1, 1)
+                    start = k * u if tile == 0 else before[t]
+                    change += flux - jnp.where(first_lane, start, turned)
+                    before[t] = turned
+                    field[later, x, cut, lanes] = (
+                        u + 0.5 * change + r_ref[x, cut, lanes] * jnp.tanh(u))
 
         if step == 0:
             wait_halos(STEPS)
@@ -226,8 +241,6 @@
                 spot = pl.ds(t * SUB * nx + x, SUB, stride=nx)
                 tall[tile, spot, :] = value[:, tile * LANES:(tile + 1) * LANES]
 
-    lane = lax.broadcasted_iota(jnp.int32, (SUB, LANES), 1)
-
     @pl.loop(0, ny * nx // SUB, unroll=4)
     def _(block):
         spot = pl.ds(pl.multiple_of(block * SUB, SUB), SUB)
@@ -256,6 +269,7 @@
 
     def render(group, view, first):
         rate = [sgn_ref[view * ztiles + first + a] * LOG2E for a in range(WIDE)]
+        c2 = [c2_ref[b] for b in range(bumps)]
 
         def plane(y, carry):
             offset = off_ref[view, iy * ny + y]
@@ -268,11 +282,12 @@
                 turned.append(pltpu.roll(mixed, (LANES - whole) & (LANES - 1), 1))
             inside = lane < LANES - whole
             result = []
+            wop = [wop_ref[b] for b in range(bumps)]
             for a in range(WIDE):
                 sums, depth, light = carry[a]
                 s = jnp.where(inside, turned[a], turned[a + 1])
-                bump = [jnp.exp2(s * (c2_ref[b] - s)) for b in range(bumps)]
-                terms = [wop_ref[b] * bump[b] for b in range(bumps)]
+                bump = [jnp.exp2(s * (c2[b] - s)) for b in range(bumps)]
+                terms = [wop[b] * bump[b] for b in range(bumps)]
                 while len(terms) > 1:
                     terms = [i + j for i, j in zip(terms[::2], terms[1::2])]
                 depth = depth + terms[0]
@@ -406,19 +421,24 @@
 
 
 def deliver(*refs):
-    count = (len(refs) - 1) // 2
-    sem = refs[-1]
+    count = (len(refs) - 2) // 3
+    sem_in, sem_out = refs[-2:]
     copies = []
-    for src, dst in zip(refs[:count], refs[count:-1]):
+    for src, dst, held in zip(refs[:count], refs[count:2 * count], refs[2 * count:-2]):
         pieces = CHUNKS if src.shape[0] % CHUNKS == 0 else 1
         size = src.shape[0] // pieces
         for piece in range(pieces):
-            cut = pl.ds(piece * size, size)
-            copies.append(pltpu.make_async_copy(src.at[cut], dst.at[cut], sem.at[len(copies)]))
-    for copy in copies:
-        copy.start()
-    for copy in copies:
-        copy.wait()
+            cut, at = pl.ds(piece * size, size), len(copies)
+            copies.append((
+                pltpu.make_async_copy(src.at[cut], held.at[cut], sem_in.at[at]),
+                pltpu.make_async_copy(held.at[cut], dst.at[cut], sem_out.at[at])))
+    for come, _ in copies:
+        come.start()
+    for come, go in copies:
+        come.wait()
+        go.start()
+    for _, go in copies:
+        go.wait()
 
 
 def per_device(n_x, n_y, scalar_field, diffusivity, reaction_rate, shear_offsets, depth_order,
@@ -474,7 +494,8 @@
         out_shape=results,
         in_specs=[far] * 3,
         out_specs=(far,) * 3,
-        scratch_shapes=[pltpu.SemaphoreType.DMA((3 * CHUNKS,))],
+        scratch_shapes=[space(*result.shape) for result in results]
+        + [pltpu.SemaphoreType.DMA((3 * CHUNKS,))] * 2,
         compiler_params=pltpu.CompilerParams(vmem_limit_bytes=60 * 1024 * 1024),
     )(*made)
 

time: 126 us -> 92.8 us (0.74)
  Pallas kernels: 125 us -> 90.8 us
    pallas_call x1, Pallas kernels: 68.8 us -> 2.71 us  [per_device(): pl.pallas_call(deliver, out_shape=results, in_specs=[far] * 3, out_specs=...]
    pallas_call x1, Pallas kernels: 56 us -> 88.1 us  [per_device(): pl.pallas_call(functools.partial(kernel, n_x, n_y), out_shape=results, in...]
where the time goes in v4:
time: 92.8 us; the launch traced here: 91.5 us
  Pallas kernels  90.8 us (98%)
    pallas_call x1, Pallas kernels, per_device(): pl.pallas_call(functools.partial(kernel, n_x, n_y), out_shape=results, in...  88.1 us
    pallas_call x1, Pallas kernels, per_device(): pl.pallas_call(deliver, out_shape=results, in_specs=[far] * 3, out_specs=...  2.71 us

profile of v4, /device:TPU:5, one launch (start us, length us, event | category | flops | bytes accessed | tf_op | source)
XLA Modules:
  0.0 91.5 jit_solution(6483675309243632383)
XLA Ops:
  0.6 88.1 %shard_map.103 = (f32[32,32,512]{2,1,0:T(8,128)}, f32[4,3,4,512]{3,2,1,0:T(4,128)}, f32[4,4,512]{2,1,0:T(4,128)}) custom-call(f32[32,32,512]{2,1,0:T(8,128)} %u_hbm.1, f32[32,32,512]{2,1,0:T(8,128)} %d_hbm.1, f32[32,32,512]{2,1,0:T(8,128)} %r_hbm.1, s32[4,256]{1,0:T(4,128)} %off_hbm.1, s32[4,512]{1,0:T(4,128)} %ord_hbm.1, f32[8]{0:T(128)} %cen_hbm.1, ...), custom_call_target="tpu_custom_call" | custom-call | tf_op jit(solution)/shard_map/pallas_call | solution.py:466
  88.8 2.7 %shard_map.104 = (f32[32,32,512]{2,1,0:T(8,128)}, f32[4,3,4,512]{3,2,1,0:T(4,128)}, f32[4,4,512]{2,1,0:T(4,128)}) custom-call(f32[32,32,512]{2,1,0:T(8,128)} %get-tuple-element.6.refs_0_, f32[4,3,4,512]{3,2,1,0:T(4,128)} %get-tuple-element.7.refs_1_, f32[4,4,512]{2,1,0:T(4,128)} %get-tuple-element.8.refs_2_), custom_call_target="tpu_custom_call" | custom-call | tf_op jit(solution)/shard_map/pallas_call | solution.py:492

commit v5 on v3

--- a/solution.py
+++ b/solution.py
@@ -29,7 +29,7 @@
     n_x, n_y,
     u_hbm, d_hbm, r_hbm, off_hbm, ord_hbm, cen_hbm, col_hbm, opa_hbm,
     f_ref, img_ref, tr_ref,
-    field, cond, x_lo, x_hi, dx_lo, dx_hi, p_lo, p_hi, y_lo, y_hi,
+    field_a, field_b, cond, x_lo, x_hi, dx_lo, dx_hi, p_lo, p_hi, y_lo, y_hi,
     dp_lo, dp_hi, dy_lo, dy_hi, del_lo, del_hi, tall, slope,
     part, mate, both, got, sgn_ref, c2_ref, wop_ref, wcol_ref,
     d_ref, r_ref, off_ref, ord_ref, cen_ref, col_ref, opa_ref,
@@ -37,6 +37,7 @@
     out_sem, in_sem,
 ):
     nx, ny, nz = u_hbm.shape
+    fields = (field_a, field_b)
     views = ord_ref.shape[0]
     bumps = cen_ref.shape[0]
     ztiles = nz // LANES
@@ -47,7 +48,7 @@
 
     fetches = [
         pltpu.make_async_copy(src, dst, in_sem.at[i]) for i, (src, dst) in enumerate((
-            (u_hbm, field.at[0, :, pl.ds(0, ny)]), (d_hbm, d_ref), (r_hbm, r_ref),
+            (u_hbm, fields[0].at[:, pl.ds(0, ny)]), (d_hbm, d_ref), (r_hbm, r_ref),
             (off_hbm, off_ref), (ord_hbm, ord_ref), (cen_hbm, cen_ref), (col_hbm, col_ref),
             (opa_hbm, opa_ref)))
     ]
@@ -84,7 +85,7 @@
         else:
             now = step % 2
             src = [
-                field.at[now, 0, pl.ds(0, ny)], field.at[now, nx - 1, pl.ds(0, ny)],
+                fields[now].at[0, pl.ds(0, ny)], fields[now].at[nx - 1, pl.ds(0, ny)],
                 p_lo.at[step], p_hi.at[step],
             ][side]
             dst, own = landings[there].at[step], landings[here].at[step]
@@ -123,7 +124,7 @@
     def _(block):
         base = pl.multiple_of(block * SUB, SUB)
         for ref, row, out in (
-            (field.at[0], 0, p_lo.at[0]), (field.at[0], ny - 1, p_hi.at[0]),
+            (fields[0], 0, p_lo.at[0]), (fields[0], ny - 1, p_hi.at[0]),
             (d_ref, 0, dp_lo), (d_ref, ny - 1, dp_hi),
         ):
             out[pl.ds(base, SUB), :] = jnp.concatenate(
@@ -144,7 +145,7 @@
         def _(x):
             for t in range(ny // SUB):
                 cut = pl.ds(t * SUB, SUB)
-                cond[x, cut, :] = conduct(d_ref[x, cut, :], field[now, x, cut, :])
+                cond[x, cut, :] = conduct(d_ref[x, cut, :], fields[now][x, cut, :])
 
         if step == 0:
             fetches[2].wait()
@@ -154,15 +155,15 @@
             below, above = jnp.maximum(x - 1, 0), jnp.minimum(x + 1, nx - 1)
             tiles = ny // SUB
             cuts = [pl.ds(t * SUB, SUB) for t in range(tiles)]
-            us = [field[now, x, cut, :] for cut in cuts]
+            us = [fields[now][x, cut, :] for cut in cuts]
             ks = [cond[x, cut, :] for cut in cuts]
             up_u = [pltpu.roll(u, SUB - 1, 0) for u in us]
             up_k = [pltpu.roll(k, SUB - 1, 0) for k in ks]
-            carried = None
+            carried, made = None, []
             for t, cut in enumerate(cuts):
                 u, k = us[t], ks[t]
-                change = (k + cond[below, cut, :]) * (field[now, below, cut, :] - u)
-                change += (k + cond[above, cut, :]) * (field[now, above, cut, :] - u)
+                change = (k + cond[below, cut, :]) * (fields[now][below, cut, :] - u)
+                change += (k + cond[above, cut, :]) * (fields[now][above, cut, :] - u)
                 if t < tiles - 1:
                     next_u = jnp.where(row_at == SUB - 1, up_u[t + 1], up_u[t])
                     next_k = jnp.where(row_at == SUB - 1, up_k[t + 1], up_k[t])
@@ -178,7 +179,9 @@
                 right_u, right_k = pltpu.roll(u, nz - 1, 1), pltpu.roll(k, nz - 1, 1)
                 flux = jnp.where(col_at == nz - 1, -ku, (k + right_k) * (right_u - u))
                 change += flux - jnp.where(col_at == 0, ku, pltpu.roll(flux, 1, 1))
-                field[later, x, cut, :] = u + 0.5 * change + r_ref[x, cut, :] * jnp.tanh(u)
+                made.append(u + 0.5 * change + r_ref[x, cut, :] * jnp.tanh(u))
+            for cut, value in zip(cuts, made):
+                fields[later][x, cut, :] = value
 
         if step == 0:
             wait_halos(STEPS)
@@ -186,9 +189,9 @@
         inner = pl.ds(0, ny)
         for x, land, diff in ((0, x_lo, dx_lo), (nx - 1, x_hi, dx_hi)):
             beside = land[step]
-            field[later, x, inner, :] += (
+            fields[later][x, inner, :] += (
                 0.5 * (cond[x, inner, :] + conduct(diff[...], beside))
-                * (beside - field[now, x, inner, :]))
+                * (beside - fields[now][x, inner, :]))
         for packed, own, land, diff, out in (
             (p_lo, dp_lo, y_lo, dy_lo, del_lo), (p_hi, dp_hi, y_hi, dy_hi, del_hi),
         ):
@@ -200,11 +203,11 @@
             base = pl.multiple_of(block * SUB, SUB)
             for packed, delta, row in ((p_lo, del_lo, 0), (p_hi, del_hi, ny - 1)):
                 extra = delta[pl.ds(base, SUB), :]
-                edge = []
+                edge = [
+                    fields[later][base + j, row:row + 1, :] + extra[j:j + 1, :]
+                    for j in range(SUB)]
                 for j in range(SUB):
-                    value = field[later, base + j, row:row + 1, :] + extra[j:j + 1, :]
-                    field[later, base + j, row:row + 1, :] = value
-                    edge.append(value)
+                    fields[later][base + j, row:row + 1, :] = edge[j]
                 if step < STEPS - 1:
                     packed[step + 1, pl.ds(base, SUB), :] = jnp.concatenate(edge, axis=0)
 
@@ -212,7 +215,7 @@
             start_halos(step + 1)
 
     last = STEPS % 2
-    out_copy = pltpu.make_async_copy(field.at[last, :, pl.ds(0, ny)], f_ref, out_sem)
+    out_copy = pltpu.make_async_copy(fields[last].at[:, pl.ds(0, ny)], f_ref, out_sem)
     out_copy.start()
 
     for ref in (tall, slope):
@@ -221,7 +224,7 @@
     @pl.loop(0, nx, unroll=2)
     def _(x):
         for t in range(ny // SUB):
-            value = field[last, x, pl.ds(t * SUB, SUB), :] * SCALE
+            value = fields[last][x, pl.ds(t * SUB, SUB), :] * SCALE
             for tile in range(ztiles):
                 spot = pl.ds(t * SUB * nx + x, SUB, stride=nx)
                 tall[tile, spot, :] = value[:, tile * LANES:(tile + 1) * LANES]
@@ -406,19 +409,24 @@
 
 
 def deliver(*refs):
-    count = (len(refs) - 1) // 2
-    sem = refs[-1]
+    count = (len(refs) - 2) // 3
+    sem_in, sem_out = refs[-2:]
     copies = []
-    for src, dst in zip(refs[:count], refs[count:-1]):
+    for src, dst, held in zip(refs[:count], refs[count:2 * count], refs[2 * count:-2]):
         pieces = CHUNKS if src.shape[0] % CHUNKS == 0 else 1
         size = src.shape[0] // pieces
         for piece in range(pieces):
-            cut = pl.ds(piece * size, size)
-            copies.append(pltpu.make_async_copy(src.at[cut], dst.at[cut], sem.at[len(copies)]))
-    for copy in copies:
-        copy.start()
-    for copy in copies:
-        copy.wait()
+            cut, at = pl.ds(piece * size, size), len(copies)
+            copies.append((
+                pltpu.make_async_copy(src.at[cut], held.at[cut], sem_in.at[at]),
+                pltpu.make_async_copy(held.at[cut], dst.at[cut], sem_out.at[at])))
+    for come, _ in copies:
+        come.start()
+    for come, go in copies:
+        come.wait()
+        go.start()
+    for _, go in copies:
+        go.wait()
 
 
 def per_device(n_x, n_y, scalar_field, diffusivity, reaction_rate, shear_offsets, depth_order,
@@ -449,7 +457,7 @@
         in_specs=[pinned] * 8,
         out_specs=(far, vmem, vmem),
         scratch_shapes=[
-            space(2, nx, ny + SUB, nz), space(nx, ny + SUB, nz),
+            space(nx, ny, nz), space(nx, ny, nz), space(nx, ny, nz),
             x_faces, x_faces, x_face, x_face,
             y_faces, y_faces, y_faces, y_faces,
             y_face, y_face, y_face, y_face, y_face, y_face,
@@ -474,7 +482,8 @@
         out_shape=results,
         in_specs=[far] * 3,
         out_specs=(far,) * 3,
-        scratch_shapes=[pltpu.SemaphoreType.DMA((3 * CHUNKS,))],
+        scratch_shapes=[space(*result.shape) for result in results]
+        + [pltpu.SemaphoreType.DMA((3 * CHUNKS,))] * 2,
         compiler_params=pltpu.CompilerParams(vmem_limit_bytes=60 * 1024 * 1024),
     )(*made)
 

time: 126 us -> 62.4 us (0.50)
  Pallas kernels: 125 us -> 61.4 us
    pallas_call x1, Pallas kernels: 68.8 us -> 2.71 us  [per_device(): pl.pallas_call(deliver, out_shape=results, in_specs=[far] * 3, out_specs=...]
    pallas_call x1, Pallas kernels: 56 us -> 58.7 us  [per_device(): pl.pallas_call(functools.partial(kernel, n_x, n_y), out_shape=results, in...]
where the time goes in v5:
time: 62.4 us; the launch traced here: 62.1 us
  Pallas kernels  61.4 us (98%)
  between operations  0.64 us (1%)
    pallas_call x1, Pallas kernels, per_device(): pl.pallas_call(functools.partial(kernel, n_x, n_y), out_shape=results, in...  58.7 us
    pallas_call x1, Pallas kernels, per_device(): pl.pallas_call(deliver, out_shape=results, in_specs=[far] * 3, out_specs=...  2.71 us

profile of v5, /device:TPU:5, one launch (start us, length us, event | category | flops | bytes accessed | tf_op | source)
XLA Modules:
  0.0 62.1 jit_solution(811744852282154891)
XLA Ops:
  0.6 58.7 %shard_map.103 = (f32[32,32,512]{2,1,0:T(8,128)}, f32[4,3,4,512]{3,2,1,0:T(4,128)}, f32[4,4,512]{2,1,0:T(4,128)}) custom-call(f32[32,32,512]{2,1,0:T(8,128)} %u_hbm.1, f32[32,32,512]{2,1,0:T(8,128)} %d_hbm.1, f32[32,32,512]{2,1,0:T(8,128)} %r_hbm.1, s32[4,256]{1,0:T(4,128)} %off_hbm.1, s32[4,512]{1,0:T(4,128)} %ord_hbm.1, f32[8]{0:T(128)} %cen_hbm.1, ...), custom_call_target="tpu_custom_call" | custom-call | tf_op jit(solution)/shard_map/pallas_call | solution.py:454
  59.4 2.7 %shard_map.104 = (f32[32,32,512]{2,1,0:T(8,128)}, f32[4,3,4,512]{3,2,1,0:T(4,128)}, f32[4,4,512]{2,1,0:T(4,128)}) custom-call(f32[32,32,512]{2,1,0:T(8,128)} %get-tuple-element.6.refs_0_, f32[4,3,4,512]{3,2,1,0:T(4,128)} %get-tuple-element.7.refs_1_, f32[4,4,512]{2,1,0:T(4,128)} %get-tuple-element.8.refs_2_), custom_call_target="tpu_custom_call" | custom-call | tf_op jit(solution)/shard_map/pallas_call | solution.py:480
